TPU v7x, 32 devices: a whole 2x2x4 slice. The times are simulated.
32 devices in a mesh: sec: 4 (over y, x), tile: 4 (over z), half: 2 (over core).
Axes of the slice: x: 2, y: 2, z: 4, core: 2. Of those that a mesh axis runs over, the one named last changes fastest.
Arguments:
- sections_in: bfloat16 [8, 256, 1024], P('sec', 'tile', 'half'), parts along dimension 2, may hold values from -30 to 30
- first_kernel: bfloat16 [12, 1, 3, 3, 3], replicated, may hold values from -1.25 to 1.25
- first_bias: float32 [12], replicated, may hold values from -3 to 3
- second_kernel: bfloat16 [12, 12, 3, 3, 3], replicated, may hold values from -0.3125 to 0.3125
- second_bias: float32 [12], replicated, may hold values from -3 to 3
- head_kernel: bfloat16 [3, 12], replicated, may hold values from -1.75 to 1.75
- head_bias: float32 [3], replicated, may hold values from -3 to 3
Outputs:
- affinity: float32 [3, 8, 256, 1024], P(None, None, 'sec', ('half', 'tile')), parts along dimension 3
There are 2 independent parts, one for each index of `half`. A program takes and returns all parts, laid end to end along the dimension named above; an argument that names none is the same for every part. Nothing has to cross between parts.
All inputs are finite; a program needn't handle non-finite values.
Results may differ from a plain program's by a relative error of at most 0.0016.
Values may be sent and summed in bfloat16 or wider, within the bound.
A program may use at most 128 MiB of HBM per device.

v0:
```python
import jax
import jax.numpy as jnp
from jax import lax
from jax.sharding import PartitionSpec as P


def padded_2(shard, sides, width):
    for axis, dim in sides:
        peers, length = (lax.axis_size(axis), shard.shape[dim])
        up = [(i, (i + 1) % peers) for i in range(peers - 1)]
        down = [(j, i) for i, j in up]
        last = lax.slice_in_dim(shard, length - width, length, axis=dim)
        initial = lax.slice_in_dim(shard, 0, width, axis=dim)
        before = lax.ppermute(last, axis, up)
        after = lax.ppermute(initial, axis, down)
        shard = jnp.concatenate([before, shard, after], axis=dim)
    return shard


def convolve(volume, kernel, padding):
    return lax.conv_general_dilated(
        volume,
        kernel,
        (1, 1, 1),
        padding,
        dimension_numbers=("NCDHW", "OIDHW", "NCDHW"),
        preferred_element_type=jnp.float32,
    )


def activate(summed, bias):
    return jax.nn.relu(summed + bias[None, :, None, None, None]).astype(jnp.bfloat16)


def local_sums(volume):
    values = volume.astype(jnp.float32)
    return (jnp.sum(values, axis=(1, 2)), jnp.sum(values * values, axis=(1, 2)))


def normalize(volume, first_sum, second_sum, cells_total):
    average = first_sum / cells_total
    variance = second_sum / cells_total - average * average
    inv_std = lax.rsqrt(variance + 1e-05)
    shifted = volume.astype(jnp.float32) - average[:, None, None]
    return (shifted * inv_std[:, None, None]).astype(jnp.bfloat16)


def brick_normalize(volume):
    plain_sum, square_sum = local_sums(volume)
    first_sum, second_sum = lax.psum((plain_sum, square_sum), ("sec", "tile"))
    cells_total = volume.shape[1] * volume.shape[2] * lax.axis_size("sec") * lax.axis_size("tile")
    return normalize(volume, first_sum, second_sum, cells_total)


def regroup(volume):
    return lax.all_to_all(
        lax.all_to_all(volume, "tile", split_axis=2, concat_axis=1, tiled=True),
        "sec",
        split_axis=1,
        concat_axis=0,
        tiled=True,
    )


def finish(widened, second_kernel, second_bias, head_kernel, head_bias):
    second_out = activate(
        convolve(widened[None], second_kernel, ((1, 1), (0, 0), (0, 0))), second_bias
    )
    logits = jnp.einsum(
        "oc,czyx->ozyx", head_kernel, second_out[0], preferred_element_type=jnp.float32
    )
    return jax.nn.sigmoid(logits + head_bias[:, None, None, None])


def per_device(
    sections_in, first_kernel, first_bias, second_kernel, second_bias, head_kernel, head_bias
):
    level = ((1, 1), (0, 0), (0, 0))
    brick = brick_normalize(regroup(sections_in))
    padded = padded_2(brick, (("sec", 1), ("tile", 2)), 2)
    first_out = activate(convolve(padded[None, None], first_kernel, level), first_bias)[0]
    rows_here = brick.shape[1]
    cols_here = brick.shape[2]
    row_index = lax.axis_index("sec") * rows_here - 1 + jnp.arange(rows_here + 2, dtype=jnp.int32)
    col_index = lax.axis_index("tile") * cols_here - 1 + jnp.arange(cols_here + 2, dtype=jnp.int32)
    row_inside = (row_index >= 0) & (row_index < rows_here * lax.axis_size("sec"))
    col_inside = (col_index >= 0) & (col_index < cols_here * lax.axis_size("tile"))
    inside = row_inside[:, None] & col_inside[None, :]
    widened = jnp.where(inside[None, None], first_out, jnp.zeros((), jnp.bfloat16))
    return finish(widened, second_kernel, second_bias, head_kernel, head_bias)


def solution(mesh):
    in_specs = (P("sec", "tile", "half"), P(), P(), P(), P(), P(), P())
    out_specs = P(None, None, "sec", ("half", "tile"))
    return jax.shard_map(
        per_device, mesh=mesh, in_specs=in_specs, out_specs=out_specs, check_vma=False
    )
```

profile of v0, /device:TPU:0, one launch (start us, length us, event | category | flops | bytes accessed | tf_op | source)
XLA Modules:
  0.0 273.2 jit_solution(5084673572646575382)
XLA Ops:
  0.0 1.1 copy.95
  1.1 0.9 reshape.84
  2.0 6.3 %all-to-all-start = ((bf16[4,2,8192]{2,1,0:T(2,128)(2,1)}), bf16[4,2,8192]{2,1,0:T(2,128)(2,1)S(1)}, u32[]{:S(2)}, u32[]{:S(2)}) async-start(bf16[4,2,8192]{2,1,0:T(2,128)(2,1)} %reshape.84), calls=%async_computation | async-start | bytes 262144 | tf_op jit(solution)/shard_map/all_to_all | solution.py:57
  8.3 6.1 %all-to-all-done = bf16[4,2,8192]{2,1,0:T(2,128)(2,1)S(1)} async-done(((bf16[4,2,8192]{2,1,0:T(2,128)(2,1)}), bf16[4,2,8192]{2,1,0:T(2,128)(2,1)S(1)}, u32[]{:S(2)}, u32[]{:S(2)}) %all-to-all-start) | async-done | bytes 131104 | tf_op jit(solution)/shard_map/all_to_all | solution.py:57
  14.4 0.2 reshape.85
  14.8 0.8 copy.98
  15.6 3.7 %all-to-all-start.1 = ((bf16[2,256,128]{2,0,1:T(2,128)(2,1)}), bf16[2,256,128]{2,0,1:T(2,128)(2,1)S(1)}, u32[]{:S(2)}, u32[]{:S(2)}) async-start(bf16[2,256,128]{2,0,1:T(2,128)(2,1)} %copy.98), calls=%async_computation.1 | async-start | bytes 262144 | tf_op jit(solution)/shard_map/all_to_all | solution.py:56
  19.3 5.0 %all-to-all-done.1 = bf16[2,256,128]{2,0,1:T(2,128)(2,1)S(1)} async-done(((bf16[2,256,128]{2,0,1:T(2,128)(2,1)}), bf16[2,256,128]{2,0,1:T(2,128)(2,1)S(1)}, u32[]{:S(2)}, u32[]{:S(2)}) %all-to-all-start.1) | async-done | bytes 131104 | tf_op jit(solution)/shard_map/all_to_all | solution.py:56
  24.9 38.3 %all-reduce = (f32[8]{0:T(128)S(1)}, f32[8]{0:T(128)S(1)}) all-reduce(f32[8]{0:T(128)S(1)} %reduce_sum.25, f32[8]{0:T(128)S(1)} %reduce_sum.23), channel_id=1, replica_groups=mesh['sec'=4,'tile'=4,'half'=2] {'sec','tile'}, use_global_device_ids=true, to_apply=%region_3.0 | all-reduce | flops 16 | bytes 128 | tf_op jit(solution)/shard_map/psum | solution.py:50
  63.4 1.3 collective-permute-start
  64.7 1.3 collective-permute-start.1
  66.0 5.9 %collective-permute-done.1 = bf16[8,2,128]{2,1,0:T(2,128)(2,1)S(1)} collective-permute-done((bf16[8,2,128]{2,1,0:T(2,128)(2,1)S(1)}, bf16[8,2,128]{2,1,0:T(2,128)(2,1)S(1)}, u32[]{:S(2)}, u32[]{:S(2)}) %collective-permute-start.1) | collective-permute-done | bytes 4128 | tf_op jit(solution)/shard_map/ppermute | solution.py:15
  72.1 1.6 collective-permute-start.2
  73.7 1.3 collective-permute-start.3
  75.1 1.3 collective-permute-done.2
  76.4 4.4 %collective-permute-done.3 = bf16[8,68,2]{2,1,0:T(8,128)(2,1)S(1)} collective-permute-done((bf16[8,68,2]{2,1,0:T(8,128)(2,1)S(1)}, bf16[8,68,2]{2,1,0:T(8,128)(2,1)S(1)}, u32[]{:S(2)}, u32[]{:S(2)}) %collective-permute-start.3) | collective-permute-done | bytes 2208 | tf_op jit(solution)/shard_map/ppermute | solution.py:15
  80.7 0.3 maximum_bitcast_fusion
  81.0 0.3 copy.120
  81.4 10.0 %copy.105 = bf16[1,8,68,8,19]{3,0,4,2,1:T(2,128)(2,1)} copy(bf16[1,8,68,8,19]{2,1,4,3,0:T(8,128)(2,1)S(1)} %fusion.34) | data formatting | bytes 330752 | tf_op jit(solution)/shard_map/conv_general_dilated | solution.py:21
  91.4 62.1 %maximum_convert_fusion = bf16[8,66,8,17,12]{4,2,3,1,0:T(8,128)(2,1)} fusion(f32[12]{0:T(128)} %param.9, pred[8,17]{0,1:T(8,128)(4,1)} %constant.50, bf16[1,8,68,8,19]{3,0,4,2,1:T(2,128)(2,1)} %copy.105, bf16[12,1,3,3,3]{0,4,3,2,1:T(4,128)(2,1)} %param.8), kind=kOutput, calls=%fused_computation.2 | convolution fusion | flops 46100736 | bytes 1889600 | tf_op jit(solution)/shard_map/conv_general_dilated | solution.py:21
  153.5 18.6 %copy.107 = bf16[8,66,8,17,12]{1,0,4,3,2:T(8,128)(2,1)S(1)} copy(bf16[8,66,8,17,12]{4,2,3,1,0:T(8,128)(2,1)} %maximum_convert_fusion) | data formatting | bytes 3446784 | tf_op jit(solution)/shard_map/convert_element_type | solution.py:32
  172.2 0.3 fusion.11
  172.5 0.5 copy.121
  173.0 0.8 pad.2.clone
  173.9 16.7 %copy.110 = bf16[12,8,66,1,8,17]{0,4,5,2,1,3:T(8,128)(2,1)} copy(bf16[12,8,66,1,8,17]{2,1,5,4,0,3:T(8,128)(2,1)S(1)} %bitcast.62) | data formatting | bytes 3446784 | tf_op jit(solution)/shard_map/conv_general_dilated | solution.py:21
  190.5 2.2 slice.26
  192.8 50.5 %maximum_convert_fusion.1 = bf16[8,64,8,17,12]{4,2,3,1,0:T(8,128)(2,1)} fusion(f32[12]{0:T(128)S(1)} %copy-done.2, pred[8,17]{0,1:T(8,128)(4,1)S(1)} %copy-done.4, bf16[12,8,66,1,7,2]{0,4,5,2,1,3:T(8,128)(2,1)S(1)} %slice.26, bf16[12,8,66,1,8,17]{0,4,5,2,1,3:T(8,128)(2,1)} %copy.110, bf16[12,12,3,3,3]{1,4,3,2,0:T(4,128)(2,1)S(1)} %copy-done), kind=kOutput, calls=%fused_computation.3 | convolution fusion | flops 505457664 | bytes 3579928 | tf_op jit(solution)/shard_map/conv_general_dilated | solution.py:21
  243.3 18.9 %copy.112 = bf16[8,64,8,17,12]{1,0,4,3,2:T(8,128)(2,1)S(1)} copy(bf16[8,64,8,17,12]{4,2,3,1,0:T(8,128)(2,1)} %maximum_convert_fusion.1) | data formatting | bytes 3342336 | tf_op jit(solution)/shard_map/convert_element_type | solution.py:32
  262.2 1.8 slice.27
  264.0 7.5 %copy.119 = bf16[8,64,1,128,12]{3,4,1,0,2:T(8,128)(2,1)S(1)} copy(bf16[8,64,1,128,12]{1,0,4,3,2:T(8,128)(2,1)} %slice.27) | data formatting | bytes 3145728
  271.6 0.7 fusion.29
  272.3 1.0 copy.114
  (31 shorter events, 1.3 us)
Async XLA Ops:
  0.0 192.7 %copy-start = (bf16[12,12,3,3,3]{1,4,3,2,0:T(4,128)(2,1)S(1)}, bf16[12,12,3,3,3]{1,4,3,2,0:T(4,128)(2,1)}, u32[]{:S(2)}) copy-start(bf16[12,12,3,3,3]{1,4,3,2,0:T(4,128)(2,1)} %param.10) | copy-start | bytes 23332
  2.0 12.4 %all-to-all-start = ((bf16[4,2,8192]{2,1,0:T(2,128)(2,1)}), bf16[4,2,8192]{2,1,0:T(2,128)(2,1)S(1)}, u32[]{:S(2)}, u32[]{:S(2)}) async-start(bf16[4,2,8192]{2,1,0:T(2,128)(2,1)} %reshape.84), calls=%async_computation | async-start | bytes 262144 | tf_op jit(solution)/shard_map/all_to_all | solution.py:57
  15.6 8.7 %all-to-all-start.1 = ((bf16[2,256,128]{2,0,1:T(2,128)(2,1)}), bf16[2,256,128]{2,0,1:T(2,128)(2,1)S(1)}, u32[]{:S(2)}, u32[]{:S(2)}) async-start(bf16[2,256,128]{2,0,1:T(2,128)(2,1)} %copy.98), calls=%async_computation.1 | async-start | bytes 262144 | tf_op jit(solution)/shard_map/all_to_all | solution.py:56
  63.4 2.6 collective-permute-start
  64.7 7.2 %collective-permute-start.1 = (bf16[8,2,128]{2,1,0:T(2,128)(2,1)S(1)}, bf16[8,2,128]{2,1,0:T(2,128)(2,1)S(1)}, u32[]{:S(2)}, u32[]{:S(2)}) collective-permute-start(bf16[8,2,128]{2,1,0:T(2,128)(2,1)S(1)} %get-tuple-element.12), channel_id=1, source_target_pairs={{8,0},{16,8},{24,16},{9,1},{17,9},{25,17},{10,2},{18,10},{26,18},{... | collective-permute-start | bytes 12296 | tf_op jit(solution)/shard_map/ppermute | solution.py:15
  72.1 4.2 %collective-permute-start.2 = (bf16[8,68,2]{2,1,0:T(8,128)(2,1)S(1)}, bf16[8,68,2]{2,1,0:T(8,128)(2,1)S(1)}, u32[]{:S(2)}, u32[]{:S(2)}) collective-permute-start(bf16[8,68,2]{2,1,0:T(8,128)(2,1)S(1)} %get-tuple-element.9), channel_id=1, source_target_pairs={{0,2},{2,4},{4,6},{1,3},{3,5},{5,7},{8,10},{10,12},{12,14},{9,11},... | collective-permute-start | bytes 6536 | tf_op jit(solution)/shard_map/ppermute | solution.py:14
  73.7 7.0 %collective-permute-start.3 = (bf16[8,68,2]{2,1,0:T(8,128)(2,1)S(1)}, bf16[8,68,2]{2,1,0:T(8,128)(2,1)S(1)}, u32[]{:S(2)}, u32[]{:S(2)}) collective-permute-start(bf16[8,68,2]{2,1,0:T(8,128)(2,1)S(1)} %get-tuple-element.10), channel_id=1, source_target_pairs={{2,0},{4,2},{6,4},{3,1},{5,3},{7,5},{10,8},{12,10},{14,12},{11,9},... | collective-permute-start | bytes 6536 | tf_op jit(solution)/shard_map/ppermute | solution.py:15
  172.4 20.3 %copy-start.2 = (f32[12]{0:T(128)S(1)}, f32[12]{0:T(128)}, u32[]{:S(2)}) copy-start(f32[12]{0:T(128)} %param.11) | copy-start | bytes 148
  172.5 20.3 %copy-start.4 = (pred[8,17]{0,1:T(8,128)(4,1)S(1)}, pred[8,17]{0,1:T(8,128)(4,1)}, u32[]{:S(2)}) copy-start(pred[8,17]{0,1:T(8,128)(4,1)} %constant.49) | copy-start | bytes 412
  243.3 28.2 %copy-start.1 = (bf16[3,12]{1,0:T(4,128)(2,1)S(1)}, bf16[3,12]{1,0:T(4,128)(2,1)}, u32[]{:S(2)}) copy-start(bf16[3,12]{1,0:T(4,128)(2,1)} %param.12) | copy-start | bytes 220
  243.3 28.2 %copy-start.3 = (f32[3]{0:T(128)S(1)}, f32[3]{0:T(128)}, u32[]{:S(2)}) copy-start(f32[3]{0:T(128)} %param.13) | copy-start | bytes 40
where the time goes:
time: 274 us; the launch traced here: 273 us
  matrix products  113 us (41%)
  local copies, waits for them, and re-layouts  82.1 us (30%)
  blocking collectives  38.3 us (14%)
  waiting for transfers between devices  22.7 us (8%)
  starting transfers between devices  15.5 us (6%)
    conv_general_dilated x2, matrix products, convolve(): lax.conv_general_dilated(volume, kernel, (1, 1, 1), padding, dimension_nu...  113 us
    convert_element_type x3, local copies, waits for them, and re-layouts, activate(): jax.nn.relu(summed + bias[None, :, None, None, None]).astype(jnp.bfloat16)  39.4 us
    psum x1, blocking collectives, brick_normalize(): first_sum, second_sum = lax.psum((plain_sum, square_sum), ('sec', 'tile'))  38.3 us
    conv_general_dilated x4, local copies, waits for them, and re-layouts, convolve(): lax.conv_general_dilated(volume, kernel, (1, 1, 1), padding, dimension_nu...  28.8 us
    unnamed x16, local copies, waits for them, and re-layouts  10.6 us
    ppermute x2, waiting for transfers between devices, padded_2(): after = lax.ppermute(initial, axis, down)  10.3 us
    all_to_all x1, starting transfers between devices, regroup(): lax.all_to_all(volume, 'tile', split_axis=2, concat_axis=1, tiled=True)  6.32 us
    all_to_all x1, waiting for transfers between devices, regroup(): lax.all_to_all(volume, 'tile', split_axis=2, concat_axis=1, tiled=True)  6.07 us
  transfers between devices with their start and end apart: 6, of which 5 were waited for; matrix products, arithmetic and copies ran while one was open for 0% of the time, Pallas kernels for 0%

commit v1 on v0

--- a/solution.py
+++ b/solution.py
@@ -47,7 +47,7 @@
 
 def brick_normalize(volume):
     plain_sum, square_sum = local_sums(volume)
-    first_sum, second_sum = lax.psum((plain_sum, square_sum), ("sec", "tile"))
+    first_sum, second_sum = lax.psum(lax.psum((plain_sum, square_sum), "tile"), "sec")
     cells_total = volume.shape[1] * volume.shape[2] * lax.axis_size("sec") * lax.axis_size("tile")
     return normalize(volume, first_sum, second_sum, cells_total)
 

time: 274 us -> 255 us (0.931)
  blocking collectives: 38.3 us -> 18.2 us
    psum x1 -> x2, blocking collectives: 38.3 us -> 18.2 us  [the longest x1 9.82 us: brick_normalize(): lax.psum((plain_sum, square_sum), 'tile')]
where the time goes in v1:
time: 255 us; the launch traced here: 254 us
  matrix products  113 us (44%)
  local copies, waits for them, and re-layouts  82.2 us (32%)
  waiting for transfers between devices  20.9 us (8%)
  blocking collectives  18.2 us (7%)
  starting transfers between devices  18 us (7%)
    conv_general_dilated x2, matrix products, convolve(): lax.conv_general_dilated(volume, kernel, (1, 1, 1), padding, dimension_nu...  113 us
    convert_element_type x3, local copies, waits for them, and re-layouts, activate(): jax.nn.relu(summed + bias[None, :, None, None, None]).astype(jnp.bfloat16)  39.4 us
    conv_general_dilated x4, local copies, waits for them, and re-layouts, convolve(): lax.conv_general_dilated(volume, kernel, (1, 1, 1), padding, dimension_nu...  28.9 us
    unnamed x16, local copies, waits for them, and re-layouts  10.6 us
    psum x1, blocking collectives, brick_normalize(): lax.psum((plain_sum, square_sum), 'tile')  9.82 us
    ppermute x2, waiting for transfers between devices, padded_2(): after = lax.ppermute(initial, axis, down)  8.56 us
    psum x1, blocking collectives, brick_normalize(): lax.psum(lax.psum((plain_sum, square_sum), 'tile'), 'sec')  8.36 us
    all_to_all x1, starting transfers between devices, regroup(): lax.all_to_all(volume, 'tile', split_axis=2, concat_axis=1, tiled=True)  6.32 us
  transfers between devices with their start and end apart: 6, of which 5 were waited for; matrix products, arithmetic and copies ran while one was open for 0% of the time, Pallas kernels for 0%

profile of v1, /device:TPU:0, one launch (start us, length us, event | category | flops | bytes accessed | tf_op | source)
XLA Modules:
  0.0 253.9 jit_solution(1500928475265500777)
XLA Ops:
  0.0 1.1 copy.95
  1.1 0.9 reshape.84
  2.0 6.3 %all-to-all-start = ((bf16[4,2,8192]{2,1,0:T(2,128)(2,1)}), bf16[4,2,8192]{2,1,0:T(2,128)(2,1)S(1)}, u32[]{:S(2)}, u32[]{:S(2)}) async-start(bf16[4,2,8192]{2,1,0:T(2,128)(2,1)} %reshape.84), calls=%async_computation | async-start | bytes 262144 | tf_op jit(solution)/shard_map/all_to_all | solution.py:57
  8.3 6.1 %all-to-all-done = bf16[4,2,8192]{2,1,0:T(2,128)(2,1)S(1)} async-done(((bf16[4,2,8192]{2,1,0:T(2,128)(2,1)}), bf16[4,2,8192]{2,1,0:T(2,128)(2,1)S(1)}, u32[]{:S(2)}, u32[]{:S(2)}) %all-to-all-start) | async-done | bytes 131104 | tf_op jit(solution)/shard_map/all_to_all | solution.py:57
  14.8 0.8 copy.98
  15.6 3.7 %all-to-all-start.1 = ((bf16[2,256,128]{2,0,1:T(2,128)(2,1)}), bf16[2,256,128]{2,0,1:T(2,128)(2,1)S(1)}, u32[]{:S(2)}, u32[]{:S(2)}) async-start(bf16[2,256,128]{2,0,1:T(2,128)(2,1)} %copy.98), calls=%async_computation.1 | async-start | bytes 262144 | tf_op jit(solution)/shard_map/all_to_all | solution.py:56
  19.3 5.0 %all-to-all-done.1 = bf16[2,256,128]{2,0,1:T(2,128)(2,1)S(1)} async-done(((bf16[2,256,128]{2,0,1:T(2,128)(2,1)}), bf16[2,256,128]{2,0,1:T(2,128)(2,1)S(1)}, u32[]{:S(2)}, u32[]{:S(2)}) %all-to-all-start.1) | async-done | bytes 131104 | tf_op jit(solution)/shard_map/all_to_all | solution.py:56
  24.9 9.8 %all-reduce = (f32[8]{0:T(128)S(1)}, f32[8]{0:T(128)S(1)}) all-reduce(f32[8]{0:T(128)S(1)} %reduce_sum.25, f32[8]{0:T(128)S(1)} %reduce_sum.23), channel_id=1, replica_groups=mesh['sec'=4,'tile'=4,'half'=2] {'tile'}, use_global_device_ids=true, to_apply=%region_4.0 | all-reduce | flops 16 | bytes 128 | tf_op jit(solution)/shard_map/psum | solution.py:50
  34.8 8.4 %all-reduce.1 = (f32[8]{0:T(128)S(1)}, f32[8]{0:T(128)S(1)}) all-reduce(f32[8]{0:T(128)S(1)} %get-tuple-element.7, f32[8]{0:T(128)S(1)} %get-tuple-element.8), channel_id=1, replica_groups=mesh['sec'=4,'tile'=4,'half'=2] {'sec'}, use_global_device_ids=true, to_apply=%region_5.0 | all-reduce | flops 16 | bytes 128 | tf_op jit(solution)/shard_map/psum | solution.py:50
  43.3 3.0 %collective-permute-start = (bf16[8,2,128]{2,1,0:T(2,128)(2,1)S(1)}, bf16[8,2,128]{2,1,0:T(2,128)(2,1)S(1)}, u32[]{:S(2)}, u32[]{:S(2)}) collective-permute-start(bf16[8,2,128]{2,1,0:T(2,128)(2,1)S(1)} %get-tuple-element.13), channel_id=1, source_target_pairs={{0,8},{8,16},{16,24},{1,9},{9,17},{17,25},{2,10},{10,18},{18,26},{... | collective-permute-start | bytes 12296 | tf_op jit(solution)/shard_map/ppermute | solution.py:14
  46.2 1.3 collective-permute-start.1
  47.6 4.2 %collective-permute-done.1 = bf16[8,2,128]{2,1,0:T(2,128)(2,1)S(1)} collective-permute-done((bf16[8,2,128]{2,1,0:T(2,128)(2,1)S(1)}, bf16[8,2,128]{2,1,0:T(2,128)(2,1)S(1)}, u32[]{:S(2)}, u32[]{:S(2)}) %collective-permute-start.1) | collective-permute-done | bytes 4128 | tf_op jit(solution)/shard_map/ppermute | solution.py:15
  51.9 2.4 collective-permute-start.2
  54.3 1.3 collective-permute-start.3
  55.7 1.3 collective-permute-done.2
  57.0 4.4 %collective-permute-done.3 = bf16[8,68,2]{2,1,0:T(8,128)(2,1)S(1)} collective-permute-done((bf16[8,68,2]{2,1,0:T(8,128)(2,1)S(1)}, bf16[8,68,2]{2,1,0:T(8,128)(2,1)S(1)}, u32[]{:S(2)}, u32[]{:S(2)}) %collective-permute-start.3) | collective-permute-done | bytes 2208 | tf_op jit(solution)/shard_map/ppermute | solution.py:15
  61.4 0.3 maximum_bitcast_fusion
  61.6 0.3 copy.120
  62.1 10.1 %copy.105 = bf16[1,8,68,8,19]{3,0,4,2,1:T(2,128)(2,1)} copy(bf16[1,8,68,8,19]{2,1,4,3,0:T(8,128)(2,1)S(1)} %fusion.34) | data formatting | bytes 330752 | tf_op jit(solution)/shard_map/conv_general_dilated | solution.py:21
  72.2 62.1 %maximum_convert_fusion = bf16[8,66,8,17,12]{4,2,3,1,0:T(8,128)(2,1)} fusion(f32[12]{0:T(128)} %param.9, pred[8,17]{0,1:T(8,128)(4,1)} %constant.50, bf16[1,8,68,8,19]{3,0,4,2,1:T(2,128)(2,1)} %copy.105, bf16[12,1,3,3,3]{0,4,3,2,1:T(4,128)(2,1)} %param.8), kind=kOutput, calls=%fused_computation.2 | convolution fusion | flops 46100736 | bytes 1889600 | tf_op jit(solution)/shard_map/conv_general_dilated | solution.py:21
  134.2 18.6 %copy.107 = bf16[8,66,8,17,12]{1,0,4,3,2:T(8,128)(2,1)S(1)} copy(bf16[8,66,8,17,12]{4,2,3,1,0:T(8,128)(2,1)} %maximum_convert_fusion) | data formatting | bytes 3446784 | tf_op jit(solution)/shard_map/convert_element_type | solution.py:32
  152.9 0.3 fusion.11
  153.2 0.5 copy.121
  153.7 0.8 pad.2.clone
  154.6 16.7 %copy.110 = bf16[12,8,66,1,8,17]{0,4,5,2,1,3:T(8,128)(2,1)} copy(bf16[12,8,66,1,8,17]{2,1,5,4,0,3:T(8,128)(2,1)S(1)} %bitcast.62) | data formatting | bytes 3446784 | tf_op jit(solution)/shard_map/conv_general_dilated | solution.py:21
  171.3 2.2 slice.26
  173.5 50.5 %maximum_convert_fusion.1 = bf16[8,64,8,17,12]{4,2,3,1,0:T(8,128)(2,1)} fusion(f32[12]{0:T(128)S(1)} %copy-done.2, pred[8,17]{0,1:T(8,128)(4,1)S(1)} %copy-done.4, bf16[12,8,66,1,7,2]{0,4,5,2,1,3:T(8,128)(2,1)S(1)} %slice.26, bf16[12,8,66,1,8,17]{0,4,5,2,1,3:T(8,128)(2,1)} %copy.110, bf16[12,12,3,3,3]{1,4,3,2,0:T(4,128)(2,1)S(1)} %copy-done), kind=kOutput, calls=%fused_computation.3 | convolution fusion | flops 505457664 | bytes 3579928 | tf_op jit(solution)/shard_map/conv_general_dilated | solution.py:21
  224.0 18.9 %copy.112 = bf16[8,64,8,17,12]{1,0,4,3,2:T(8,128)(2,1)S(1)} copy(bf16[8,64,8,17,12]{4,2,3,1,0:T(8,128)(2,1)} %maximum_convert_fusion.1) | data formatting | bytes 3342336 | tf_op jit(solution)/shard_map/convert_element_type | solution.py:32
  242.9 1.8 slice.27
  244.7 7.5 %copy.119 = bf16[8,64,1,128,12]{3,4,1,0,2:T(8,128)(2,1)S(1)} copy(bf16[8,64,1,128,12]{1,0,4,3,2:T(8,128)(2,1)} %slice.27) | data formatting | bytes 3145728
  252.2 0.7 fusion.29
  252.9 1.0 copy.114
  (32 shorter events, 1.5 us)
Async XLA Ops:
  0.0 173.5 %copy-start = (bf16[12,12,3,3,3]{1,4,3,2,0:T(4,128)(2,1)S(1)}, bf16[12,12,3,3,3]{1,4,3,2,0:T(4,128)(2,1)}, u32[]{:S(2)}) copy-start(bf16[12,12,3,3,3]{1,4,3,2,0:T(4,128)(2,1)} %param.10) | copy-start | bytes 23332
  2.0 12.4 %all-to-all-start = ((bf16[4,2,8192]{2,1,0:T(2,128)(2,1)}), bf16[4,2,8192]{2,1,0:T(2,128)(2,1)S(1)}, u32[]{:S(2)}, u32[]{:S(2)}) async-start(bf16[4,2,8192]{2,1,0:T(2,128)(2,1)} %reshape.84), calls=%async_computation | async-start | bytes 262144 | tf_op jit(solution)/shard_map/all_to_all | solution.py:57
  15.6 8.7 %all-to-all-start.1 = ((bf16[2,256,128]{2,0,1:T(2,128)(2,1)}), bf16[2,256,128]{2,0,1:T(2,128)(2,1)S(1)}, u32[]{:S(2)}, u32[]{:S(2)}) async-start(bf16[2,256,128]{2,0,1:T(2,128)(2,1)} %copy.98), calls=%async_computation.1 | async-start | bytes 262144 | tf_op jit(solution)/shard_map/all_to_all | solution.py:56
  43.3 4.3 %collective-permute-start = (bf16[8,2,128]{2,1,0:T(2,128)(2,1)S(1)}, bf16[8,2,128]{2,1,0:T(2,128)(2,1)S(1)}, u32[]{:S(2)}, u32[]{:S(2)}) collective-permute-start(bf16[8,2,128]{2,1,0:T(2,128)(2,1)S(1)} %get-tuple-element.13), channel_id=1, source_target_pairs={{0,8},{8,16},{16,24},{1,9},{9,17},{17,25},{2,10},{10,18},{18,26},{... | collective-permute-start | bytes 12296 | tf_op jit(solution)/shard_map/ppermute | solution.py:14
  46.2 5.5 %collective-permute-start.1 = (bf16[8,2,128]{2,1,0:T(2,128)(2,1)S(1)}, bf16[8,2,128]{2,1,0:T(2,128)(2,1)S(1)}, u32[]{:S(2)}, u32[]{:S(2)}) collective-permute-start(bf16[8,2,128]{2,1,0:T(2,128)(2,1)S(1)} %get-tuple-element.14), channel_id=1, source_target_pairs={{8,0},{16,8},{24,16},{9,1},{17,9},{25,17},{10,2},{18,10},{26,18},{... | collective-permute-start | bytes 12296 | tf_op jit(solution)/shard_map/ppermute | solution.py:15
  51.9 5.1 %collective-permute-start.2 = (bf16[8,68,2]{2,1,0:T(8,128)(2,1)S(1)}, bf16[8,68,2]{2,1,0:T(8,128)(2,1)S(1)}, u32[]{:S(2)}, u32[]{:S(2)}) collective-permute-start(bf16[8,68,2]{2,1,0:T(8,128)(2,1)S(1)} %get-tuple-element.11), channel_id=1, source_target_pairs={{0,2},{2,4},{4,6},{1,3},{3,5},{5,7},{8,10},{10,12},{12,14},{9,11},... | collective-permute-start | bytes 6536 | tf_op jit(solution)/shard_map/ppermute | solution.py:14
  54.3 7.0 %collective-permute-start.3 = (bf16[8,68,2]{2,1,0:T(8,128)(2,1)S(1)}, bf16[8,68,2]{2,1,0:T(8,128)(2,1)S(1)}, u32[]{:S(2)}, u32[]{:S(2)}) collective-permute-start(bf16[8,68,2]{2,1,0:T(8,128)(2,1)S(1)} %get-tuple-element.12), channel_id=1, source_target_pairs={{2,0},{4,2},{6,4},{3,1},{5,3},{7,5},{10,8},{12,10},{14,12},{11,9},... | collective-permute-start | bytes 6536 | tf_op jit(solution)/shard_map/ppermute | solution.py:15
  153.2 20.3 %copy-start.2 = (f32[12]{0:T(128)S(1)}, f32[12]{0:T(128)}, u32[]{:S(2)}) copy-start(f32[12]{0:T(128)} %param.11) | copy-start | bytes 148
  153.2 20.3 %copy-start.4 = (pred[8,17]{0,1:T(8,128)(4,1)S(1)}, pred[8,17]{0,1:T(8,128)(4,1)}, u32[]{:S(2)}) copy-start(pred[8,17]{0,1:T(8,128)(4,1)} %constant.49) | copy-start | bytes 412
  224.0 28.2 %copy-start.1 = (bf16[3,12]{1,0:T(4,128)(2,1)S(1)}, bf16[3,12]{1,0:T(4,128)(2,1)}, u32[]{:S(2)}) copy-start(bf16[3,12]{1,0:T(4,128)(2,1)} %param.12) | copy-start | bytes 220
  224.0 28.2 %copy-start.3 = (f32[3]{0:T(128)S(1)}, f32[3]{0:T(128)}, u32[]{:S(2)}) copy-start(f32[3]{0:T(128)} %param.13) | copy-start | bytes 40
